TPU v7x, 512 devices: a whole 4x8x8 slice. The times are simulated.
512 devices in a mesh: src: 32 (over z, x_lo, core), tgt: 16 (over x_hi, y).
Axes of the slice: x: 4 (x_hi: 2, x_lo: 2; x = x_hi * 2 + x_lo), y: 8, z: 8, core: 2. Of those that a mesh axis runs over, the one named last changes fastest.
Arguments:
- src_codes: bfloat16 [65536, 256], P('src'), may hold values from -127 to 127, as said below
- src_scales: bfloat16 [65536, 2], P('src'), may hold values from 0.0029907227 to 0.029907227
- log_source_mass: float32 [65536], P('src'), may hold values from -4 to 4
- tgt_codes: bfloat16 [32768, 256], P(('tgt', 'src')), may hold values from -127 to 127, as said below
- tgt_scales: bfloat16 [32768, 2], P(('tgt', 'src')), may hold values from 0.0029907227 to 0.029907227
- tgt_potential: bfloat16 [32768], P(('tgt', 'src')), may hold values from -4 to 4
- log_target_mass: float32 [32768], P(('tgt', 'src')), may hold values from -4 to 4
Outputs:
- new_source_potential: float32 [65536], P('src')
- new_target_potential: float32 [32768], P(('tgt', 'src'))
Inputs may be any that keep to these rules, and one draw needn't show every extreme that they name: `src_codes`: every entry is a whole number. `tgt_codes`: every entry is a whole number.
All inputs are finite; a program needn't handle non-finite values.
Results may differ from a plain program's by a relative error of at most 0.0004.
Values may be sent and summed in bfloat16 or wider, within the bound.
A program may use at most 64 MiB of HBM per device.

v0:
```python
import math

import jax
import jax.numpy as jnp
from jax import lax
from jax.sharding import PartitionSpec as P

SMOOTHING_TEMP = 0.25
INVERSE_TEMP = 4.0
FLOOR_VALUE = -1e30


def from_everyone(array, axis):
    length = lax.axis_size(axis)
    return lax.all_to_all(
        jnp.broadcast_to(array[None], (length, *array.shape)), axis, 0, 0, tiled=True
    )


def in_order(tiles, dim):
    tiles = jnp.moveaxis(tiles, 0, dim)
    dims = tiles.shape
    return tiles.reshape(*dims[:dim], dims[dim] * dims[dim + 1], *dims[dim + 2 :])


def collect(array, axis, dim):
    tiles = from_everyone(array, axis)
    return in_order(tiles, dim)


def side_by_side(arrays, axis, dim, along):
    widths = [math.prod(a.shape[along:]) for a in arrays]
    both = jnp.concatenate(
        [a.reshape(*a.shape[:along], w) for a, w in zip(arrays, widths)], axis=along
    )
    whole = collect(both, axis, dim)
    tiles = jnp.split(whole, [sum(widths[:k]) for k in range(1, len(widths))], axis=along)
    return tuple((b.reshape(*whole.shape[:along], *a.shape[along:]) for a, b in zip(arrays, tiles)))


def gathered_once(array, axis):
    leaves = jax.tree.leaves(array)
    order = sorted(range(len(leaves)), key=lambda k: -leaves[k].size)
    width = (1, *leaves[order[0]].shape)[-1]
    lines = [
        jnp.pad(leaves[k].reshape(-1), (0, -leaves[k].size % width)).reshape(-1, width)
        for k in order
    ]
    both, at, found = (from_everyone(jnp.concatenate(lines), axis), 0, {})
    for k, line in zip(order, lines):
        piece = both[:, at : at + len(line)].reshape(len(both), -1)
        found[k] = piece[:, : leaves[k].size].reshape(-1, *leaves[k].shape)
        at += len(line)
    numbers = iter(range(len(leaves)))
    return jax.tree.map(lambda _: found[next(numbers)], array)


def joined_by_halves(pieces, combine):
    while len(jax.tree.leaves(pieces)[0]) > 1:
        pieces = jax.vmap(combine)(
            *(jax.tree.map(lambda part: part[side::2], pieces) for side in (0, 1))
        )
    return jax.tree.map(lambda part: part[0], pieces)


def combined_all(array, axis, combine):
    pieces = gathered_once(array, axis)
    return joined_by_halves(pieces, combine)


def block_scores(source_codes, source_scales, target_codes, target_scales):
    feature_count = source_codes.shape[1]
    block_total = source_scales.shape[1]
    block_width = feature_count // block_total
    source_scales = source_scales.astype(jnp.float32)
    target_scales = target_scales.astype(jnp.float32)
    summed = jnp.zeros((source_codes.shape[0], target_codes.shape[0]), jnp.float32)
    for block_index in range(block_total):
        low_edge = block_index * block_width
        product = lax.dot_general(
            source_codes[:, low_edge : low_edge + block_width],
            target_codes[:, low_edge : low_edge + block_width],
            (((1,), (1,)), ((), ())),
            preferred_element_type=jnp.float32,
        )
        summed = summed + product * (
            source_scales[:, block_index : block_index + 1] * target_scales[:, block_index][None, :]
        )
    return summed * (1.0 / math.sqrt(feature_count))


def combine_pairs(first, second):
    joined = jnp.maximum(first[0], second[0])
    return (joined, first[1] * jnp.exp(first[0] - joined) + second[1] * jnp.exp(second[0] - joined))


def per_device(
    src_codes, src_scales, log_source_mass, tgt_codes, tgt_scales, tgt_potential, log_target_mass
):
    source_count = src_codes.shape[0]
    rows_per_block = min(128, source_count)
    block_count = source_count // rows_per_block
    code_blocks = src_codes.reshape(block_count, rows_per_block, src_codes.shape[1])
    scale_blocks = src_scales.reshape(block_count, rows_per_block, src_scales.shape[1])
    starting = (
        jnp.full((source_count,), FLOOR_VALUE, jnp.float32),
        jnp.zeros((source_count,), jnp.float32),
    )
    gathered = side_by_side((tgt_codes, tgt_scales, tgt_potential), "src", 0, 1)
    piece_codes, piece_scales, piece_shift = gathered
    shift_row = piece_shift.astype(jnp.float32)[None, :]

    def per_block(inputs):
        code_rows, scale_rows = inputs
        logits = (
            shift_row + block_scores(code_rows, scale_rows, piece_codes, piece_scales)
        ) * INVERSE_TEMP
        highest = jnp.max(logits, axis=1)
        return (highest, jnp.sum(jnp.exp(logits - highest[:, None]), axis=1))

    piece_max, piece_sum = lax.map(per_block, (code_blocks, scale_blocks))
    row_stats = combine_pairs(
        starting, (piece_max.reshape(source_count), piece_sum.reshape(source_count))
    )
    panel_codes, panel_scales = (gathered[0], gathered[1])
    row_peak_value, row_exp_sum = combined_all(row_stats, "tgt", combine_pairs)
    refreshed_source = SMOOTHING_TEMP * (log_source_mass - (row_peak_value + jnp.log(row_exp_sum)))
    potential_blocks = refreshed_source.reshape(block_count, rows_per_block)

    def per_column_block(inputs):
        code_rows, scale_rows, potential_rows = inputs
        logits = (
            potential_rows[:, None] + block_scores(code_rows, scale_rows, panel_codes, panel_scales)
        ) * INVERSE_TEMP
        block_max = jnp.max(logits, axis=0)
        return (block_max, jnp.sum(jnp.exp(logits - block_max[None, :]), axis=0))

    block_max, block_sum = lax.map(per_column_block, (code_blocks, scale_blocks, potential_blocks))
    column_top = jnp.max(block_max, axis=0)
    partial_lse = column_top + jnp.log(
        jnp.sum(block_sum * jnp.exp(block_max - column_top[None, :]), axis=0)
    )
    own_count = tgt_codes.shape[0]
    received = lax.all_to_all(
        partial_lse.reshape(lax.axis_size("src"), own_count),
        "src",
        split_axis=0,
        concat_axis=0,
        tiled=True,
    )
    joined = jnp.max(received, axis=0)
    column_log_total = joined + jnp.log(jnp.sum(jnp.exp(received - joined[None, :]), axis=0))
    refreshed_target = SMOOTHING_TEMP * (log_target_mass - column_log_total)
    return (refreshed_source, refreshed_target)


def solution(mesh):
    return jax.shard_map(
        per_device,
        mesh=mesh,
        in_specs=(
            P("src", None),
            P("src", None),
            P("src"),
            P(("tgt", "src"), None),
            P(("tgt", "src"), None),
            P(("tgt", "src")),
            P(("tgt", "src")),
        ),
        out_specs=(P("src"), P(("tgt", "src"))),
        check_vma=False,
    )
```

profile of v0, /device:TPU:1, one launch (start us, length us, event | category | flops | bytes accessed | tf_op | source)
XLA Modules:
  0.0 182.5 jit_solution(14340940086820506252)
XLA Ops:
  3.0 1.4 broadcast_in_dim.38
  4.4 12.9 %all-to-all-start = ((bf16[32,64,259]{2,1,0:T(8,128)(2,1)}), bf16[32,64,259]{2,1,0:T(8,128)(2,1)S(1)}, u32[]{:S(2)}, u32[]{:S(2)}) async-start(bf16[32,64,259]{2,1,0:T(8,128)(2,1)} %broadcast_in_dim.38), calls=%async_computation | async-start | bytes 3145728 | tf_op jit(solution)/shard_map/all_to_all | solution.py:15
  17.3 39.2 %all-to-all-done = bf16[32,64,259]{2,1,0:T(8,128)(2,1)S(1)} async-done(((bf16[32,64,259]{2,1,0:T(8,128)(2,1)}), bf16[32,64,259]{2,1,0:T(8,128)(2,1)S(1)}, u32[]{:S(2)}, u32[]{:S(2)}) %all-to-all-start) | async-done | bytes 1060896 | tf_op jit(solution)/shard_map/all_to_all | solution.py:15
  57.2 43.4 %while.24 = (s32[]{:T(128)}, f32[16,128]{1,0:T(8,128)S(1)}, f32[16,128]{1,0:T(8,128)S(1)}, f32[1,2048]{1,0:T(1,128)S(1)}, bf16[16,128,256]{2,1,0:T(8,128)(2,1)},...) while((s32[]{:T(128)}, f32[16,128]{1,0:T(8,128)S(1)}, ...), condition=%wide.region_3.4_spmd, body=%wide.region_0.3_spmd.sunk | while | flops 137101312 | bytes 5505141 | solution.py:121
  57.2 0.9 dynamic-slice_bitcast_fusion.4
  59.9 0.8 dynamic-slice_bitcast_fusion.4
  62.7 0.8 dynamic-slice_bitcast_fusion.4
  65.4 0.8 dynamic-slice_bitcast_fusion.4
  68.1 0.8 dynamic-slice_bitcast_fusion.4
  70.8 0.8 dynamic-slice_bitcast_fusion.4
  73.5 0.8 dynamic-slice_bitcast_fusion.4
  76.2 0.8 dynamic-slice_bitcast_fusion.4
  79.0 0.8 dynamic-slice_bitcast_fusion.4
  81.7 0.8 dynamic-slice_bitcast_fusion.4
  84.4 0.8 dynamic-slice_bitcast_fusion.4
  87.1 0.8 dynamic-slice_bitcast_fusion.4
  89.8 0.8 dynamic-slice_bitcast_fusion.4
  92.5 0.8 dynamic-slice_bitcast_fusion.4
  95.2 0.8 dynamic-slice_bitcast_fusion.4
  98.0 0.8 dynamic-slice_bitcast_fusion.4
  101.5 9.2 %all-to-all-start.1 = ((f32[16,2,2048]{2,1,0:T(2,128)}), f32[16,2,2048]{2,1,0:T(2,128)S(1)}, u32[]{:S(2)}, u32[]{:S(2)}) async-start(f32[16,2,2048]{2,1,0:T(2,128)} %broadcast_in_dim.41), calls=%async_computation.1 | async-start | bytes 524288 | tf_op jit(solution)/shard_map/all_to_all | solution.py:15
  110.8 10.3 %all-to-all-done.1 = f32[16,2,2048]{2,1,0:T(2,128)S(1)} async-done(((f32[16,2,2048]{2,1,0:T(2,128)}), f32[16,2,2048]{2,1,0:T(2,128)S(1)}, u32[]{:S(2)}, u32[]{:S(2)}) %all-to-all-start.1) | async-done | bytes 262176 | tf_op jit(solution)/shard_map/all_to_all | solution.py:15
  121.9 46.4 %while.25 = (s32[]{:T(128)}, f32[16,2048]{1,0:T(8,128)S(1)}, f32[16,2048]{1,0:T(8,128)S(1)}, f32[16,128]{1,0:T(8,128)S(1)}, bf16[16,128,256]{2,1,0:T(8,128)(2,1)...) while((s32[]{:T(128)}, f32[16,2048]{1,0:T(8,128)S(1)}, ...), condition=%wide.region_7.8_spmd, body=%wide.region_4.7_spmd.sunk | while | flops 137097472 | bytes 5552249 | solution.py:138
  121.9 0.8 dynamic-slice_bitcast_fusion.5
  124.8 0.8 dynamic-slice_bitcast_fusion.5
  127.7 0.8 dynamic-slice_bitcast_fusion.5
  130.6 0.8 dynamic-slice_bitcast_fusion.5
  133.5 0.8 dynamic-slice_bitcast_fusion.5
  136.4 0.8 dynamic-slice_bitcast_fusion.5
  139.3 0.8 dynamic-slice_bitcast_fusion.5
  162.6 0.8 dynamic-slice_bitcast_fusion.5
  168.5 13.3 %all_to_all.19 = f32[32,1,64]{2,1,0:T(1,128)S(1)} all-to-all(f32[32,1,64]{2,1,0:T(1,128)S(1)} %add.85), channel_id=1, replica_groups=mesh['src'=32,'tgt'=16] {'src'}, dimensions={0} | all-to-all | bytes 16384 | tf_op jit(solution)/shard_map/all_to_all | solution.py:144
  (326 shorter events, 73.6 us)
Async XLA Ops:
  4.4 52.1 %all-to-all-start = ((bf16[32,64,259]{2,1,0:T(8,128)(2,1)}), bf16[32,64,259]{2,1,0:T(8,128)(2,1)S(1)}, u32[]{:S(2)}, u32[]{:S(2)}) async-start(bf16[32,64,259]{2,1,0:T(8,128)(2,1)} %broadcast_in_dim.38), calls=%async_computation | async-start | bytes 3145728 | tf_op jit(solution)/shard_map/all_to_all | solution.py:15
  101.5 20.4 %copy-start = (f32[2048]{0:T(1024)S(1)}, f32[2048]{0:T(1024)}, u32[]{:S(2)}) copy-start(f32[2048]{0:T(1024)} %param.13) | copy-start | bytes 24580
  101.5 19.5 %all-to-all-start.1 = ((f32[16,2,2048]{2,1,0:T(2,128)}), f32[16,2,2048]{2,1,0:T(2,128)S(1)}, u32[]{:S(2)}, u32[]{:S(2)}) async-start(f32[16,2,2048]{2,1,0:T(2,128)} %broadcast_in_dim.41), calls=%async_computation.1 | async-start | bytes 524288 | tf_op jit(solution)/shard_map/all_to_all | solution.py:15
  121.9 60.0 %copy-start.2 = (f32[64]{0:T(128)S(1)}, f32[64]{0:T(128)}, u32[]{:S(2)}) copy-start(f32[64]{0:T(128)} %param.17) | copy-start | bytes 772
  168.3 14.1 %copy-start.1 = (f32[16,128]{1,0:T(8,128)}, f32[16,128]{1,0:T(8,128)S(1)}, u32[]{:S(2)}) copy-start(f32[16,128]{1,0:T(8,128)S(1)} %get-tuple-element.417) | copy-start | bytes 24580
where the time goes:
time: 185 us; the launch traced here: 182 us
  waiting for transfers between devices  49.4 us (27%)
  local copies, waits for them, and re-layouts  40.5 us (22%)
  other arithmetic  30.7 us (17%)
  matrix products  24.2 us (13%)
  starting transfers between devices  22.1 us (12%)
  blocking collectives  13.3 us (7%)
    all_to_all x2, waiting for transfers between devices, from_everyone(): lax.all_to_all(jnp.broadcast_to(array[None], (length, *array.shape)), axi...  49.4 us
    squeeze x32, local copies, waits for them, and re-layouts, per_device(): piece_max, piece_sum = lax.map(per_block, (code_blocks, scale_blocks))  27.2 us
    dot_general x64, matrix products, block_scores(): lax.dot_general(source_codes[:, low_edge:low_edge + block_width], target_...  24.2 us
    all_to_all x2, starting transfers between devices, from_everyone(): lax.all_to_all(jnp.broadcast_to(array[None], (length, *array.shape)), axi...  22.1 us
    convert_element_type x32, other arithmetic, block_scores(): source_scales = source_scales.astype(jnp.float32)  21 us
    all_to_all x1, blocking collectives, per_device(): lax.all_to_all(partial_lse.reshape(lax.axis_size('src'), own_count), 'src...  13.3 us
    dynamic_update_slice x32, local copies, waits for them, and re-layouts, per_device(): lax.map(per_column_block, (code_blocks, scale_blocks, potential_blocks))  6.55 us
    reduce_sum x16, other arithmetic, per_block(): return (highest, jnp.sum(jnp.exp(logits - highest[:, None]), axis=1))  4.91 us
  transfers between devices with their start and end apart: 2, of which 2 were waited for; matrix products, arithmetic and copies ran while one was open for 0% of the time, Pallas kernels for 0%

commit v1 on v0

v1 whole, which is shorter than its diff:
```python
import math

import jax
import jax.numpy as jnp
from jax import lax
from jax.experimental import pallas as pl
from jax.experimental.pallas import tpu as pltpu
from jax.sharding import PartitionSpec as P

F32 = jnp.float32
BF16 = jnp.bfloat16
NT = (((1,), (1,)), ((), ()))
NN = (((1,), (0,)), ((), ()))
MESH = pl.DeviceIdType.MESH

LOG2E = math.log2(math.e)
LN2 = math.log(2.0)
INV_TEMP = 4.0
TEMP = 0.25

SRC = 32
TGT = 16
ROWS = 2048
OWN = 64
ZS = 8


def tree(op, items):
    items = list(items)
    while len(items) > 1:
        items = [
            op(items[i], items[i + 1]) if i + 1 < len(items) else items[i]
            for i in range(0, len(items), 2)
        ]
    return items[0]


def replicate(rows):
    size = rows[0][1]
    lane = lax.broadcasted_iota(jnp.int32, (size, 128), 1)
    down = lax.broadcasted_iota(jnp.int32, (size, 128), 0)
    left = jnp.concatenate(
        [
            jnp.where(lane == down, jnp.broadcast_to(row, (size, 128)), 0.0).astype(BF16)
            for row, _ in rows
        ],
        axis=0,
    )
    return lax.dot_general(left, jnp.ones((128, 128), BF16), NN, preferred_element_type=F32)


def kernel(
    codes_ref,
    sscale_ref,
    smass_ref,
    tcodes_ref,
    tscale_ref,
    tpot_ref,
    tmass_ref,
    u_ref,
    v_ref,
    held,
    aux,
    left,
    right,
    logits,
    peak,
    total,
    scale_row,
    shift_row,
    t_scale,
    t_pot,
    lane_peak,
    lane_sum,
    row_lse,
    col_mine,
    col_lse,
    held_recv,
    aux_recv,
    row_recv,
    col_recv,
    send,
):
    src = lax.axis_index("src")
    tgt = lax.axis_index("tgt")
    z, x, core = src // 4, (src // 2) % 2, src % 2

    def slot(zz, xx, cc):
        return ((zz + 2 * ZS) % ZS) * 4 + xx * 2 + cc

    def codes_copy(piece, to):
        return pltpu.make_async_remote_copy(
            src_ref=held.at[piece],
            dst_ref=held.at[piece],
            send_sem=send.at[0],
            recv_sem=held_recv.at[piece],
            device_id={"src": to},
            device_id_type=MESH,
        )

    def aux_copy(piece, to):
        return pltpu.make_async_remote_copy(
            src_ref=aux.at[piece],
            dst_ref=aux.at[piece],
            send_sem=send.at[1],
            recv_sem=aux_recv.at[piece],
            device_id={"src": to},
            device_id_type=MESH,
        )

    def push(piece, to):
        codes_copy(piece, to).start()
        aux_copy(piece, to).start()

    def arrived(piece):
        codes_copy(piece, src).wait_recv()
        aux_copy(piece, src).wait_recv()

    up, down = slot(z + 1, x, core), slot(z - 1, x, core)
    partner, sibling = slot(z, 1 - x, core), slot(z, x, 1 - core)

    barrier = pltpu.get_barrier_semaphore()

    def greet_src(k, _):
        pl.semaphore_signal(
            barrier, inc=1, device_id={"src": (src + k) % SRC}, device_id_type=MESH
        )
        return 0

    def greet_tgt(k, _):
        pl.semaphore_signal(
            barrier, inc=1, device_id={"tgt": (tgt + k) % TGT}, device_id_type=MESH
        )
        return 0

    lax.fori_loop(1, SRC, greet_src, 0)
    lax.fori_loop(1, TGT, greet_tgt, 0)

    held[src] = tcodes_ref[...]
    own_scale = tscale_ref[...].astype(F32)
    own_pot = tpot_ref[...].astype(F32)
    blank = jnp.zeros((1, OWN), F32)
    aux[src] = jnp.concatenate(
        [own_scale[0:1], blank, own_scale[1:2], blank, own_pot, blank], axis=1
    )

    pl.semaphore_wait(barrier, SRC + TGT - 2)

    push(src, up)
    push(src, down)
    push(src, partner)
    push(src, sibling)

    source_scale = sscale_ref[...].astype(F32)

    def source_part(first, last):
        rows = [
            (source_scale[b : b + 1, k * 128 : k * 128 + 128], 128)
            for b in range(2)
            for k in range(first, last)
        ]
        wide = replicate(rows)
        many = (last - first) * 128
        ratio = wide[many:] / wide[:many]
        at = slice(first * 128, last * 128)
        scaled = codes_ref[at, 128:256].astype(F32) * ratio
        high = scaled.astype(BF16)
        left[at, 0:128] = codes_ref[at, 0:128]
        left[at, 128:256] = high
        left[at, 256:384] = high
        left[at, 384:512] = (scaled - high.astype(F32)).astype(BF16)

    source_part(0, 8)

    arrived(partner)
    push(partner, up)
    push(partner, down)
    push(partner, sibling)
    for side, onward in ((-1, up), (1, down)):
        piece = slot(z + side, x, core)
        arrived(piece)
        push(piece, onward)
        push(piece, sibling)

    source_part(8, 16)
    scale_row[...] = jnp.broadcast_to(source_scale[0:1] * (INV_TEMP * LOG2E / 16.0), (8, ROWS))
    peak[...] = jnp.full((8, ROWS), -1e30, F32)
    total[...] = jnp.zeros((8, ROWS), F32)

    for side, onward in ((-1, up), (1, down)):
        piece = slot(z + side, 1 - x, core)
        arrived(piece)
        push(piece, onward)
        push(piece, sibling)

    def chunk(k, _):
        far = (k + 1) // 2 + 1
        own_column = k % 2 == 1

        @pl.when(jnp.logical_and(k >= 1, k <= 2))
        def _():
            xx = jnp.where(own_column, x, 1 - x)
            for side, onward in ((-1, up), (1, down)):
                piece = slot(z + side * 2, xx, core)
                arrived(piece)
                push(piece, onward)
                push(piece, sibling)

        @pl.when(jnp.logical_and(k >= 3, k <= 4))
        def _():
            xx = jnp.where(own_column, x, 1 - x)
            for side, onward in ((-1, up), (1, down)):
                piece = slot(z + side * 3, xx, core)
                arrived(piece)

                @pl.when(own_column if side == -1 else jnp.logical_not(own_column))
                def _():
                    push(piece, onward)

                push(piece, sibling)

        @pl.when(k == 5)
        def _():
            for xx in (x, 1 - x):
                piece = slot(z + 4, xx, core)
                arrived(piece)
                push(piece, sibling)

        away = (k + 1) // 2
        zz = (z + jnp.where(k % 2 == 1, away, -away) + 2 * ZS) % ZS
        for xx in (0, 1):
            arrived(slot(zz, xx, 1 - core))

        first = pl.multiple_of(zz * 256, 256)
        side_rows = [aux[zz * 4 + p] for p in range(4)]
        wide = replicate(
            [(row[:, b * 128 : b * 128 + 128], OWN) for b in range(3) for row in side_rows]
        )
        t_scale[...] = wide[0:256]
        t_pot[...] = wide[512:768] * (INV_TEMP * LOG2E)
        pieces = held[pl.ds(zz * 4, 4)].reshape(256, 256)
        scaled = pieces[:, 128:256].astype(F32) * (wide[256:512] / wide[0:256])
        high = scaled.astype(BF16)
        right[:, 0:128] = pieces[:, 0:128]
        right[:, 128:256] = high
        right[:, 256:384] = (scaled - high.astype(F32)).astype(BF16)
        right[:, 384:512] = high

        for n in range(8):
            product = lax.dot_general(
                right[...], left[n * 256 : n * 256 + 256, :], NT, preferred_element_type=F32
            )
            tiles = [slice((2 * n + i) * 128, (2 * n + i) * 128 + 128) for i in range(2)]
            s_scale = [scale_row[:, t] for t in tiles]
            high_mark = [peak[:, t] for t in tiles]
            summed = [total[:, t] for t in tiles]
            for g0 in range(0, 32, 4):
                values = [[], []]
                for g in range(g0, g0 + 4):
                    down8 = slice(g * 8, g * 8 + 8)
                    scale, pot = t_scale[down8, :], t_pot[down8, :]
                    for i, t in enumerate(tiles):
                        value = product[down8, i * 128 : i * 128 + 128] * s_scale[i] * scale + pot
                        logits[pl.ds(first + g * 8, 8), t] = value
                        values[i].append(value)
                for i in range(2):
                    mark = jnp.maximum(high_mark[i], tree(jnp.maximum, values[i]))
                    added = tree(jnp.add, [jnp.exp2(value - mark) for value in values[i]])
                    summed[i] = summed[i] * jnp.exp2(high_mark[i] - mark) + added
                    high_mark[i] = mark
            for i, t in enumerate(tiles):
                peak[:, t] = high_mark[i]
                total[:, t] = summed[i]
        return 0

    lax.fori_loop(0, ZS, chunk, 0)

    for k in range(16):
        t = slice(k * 128, k * 128 + 128)
        mark = jnp.max(peak[:, t], axis=0, keepdims=True)
        row_sum = jnp.sum(total[:, t] * jnp.exp2(peak[:, t] - mark), axis=0, keepdims=True)
        row_lse[tgt, k : k + 1, :] = mark + jnp.log2(row_sum)

    def row_copy(group, to):
        return pltpu.make_async_remote_copy(
            src_ref=row_lse.at[group],
            dst_ref=row_lse.at[group],
            send_sem=send.at[2],
            recv_sem=row_recv.at[group],
            device_id={"tgt": to},
            device_id_type=MESH,
        )

    def row_push(k, _):
        row_copy(tgt, (tgt + k) % TGT).start()
        return 0

    def row_wait(k, _):
        row_copy((tgt + k) % TGT, tgt).wait_recv()
        return 0

    lax.fori_loop(1, TGT, row_push, 0)
    lax.fori_loop(1, TGT, row_wait, 0)

    every = [row_lse[g] for g in range(TGT)]
    mark = tree(jnp.maximum, every)
    joined = mark + jnp.log2(tree(jnp.add, [jnp.exp2(one - mark) for one in every]))
    mass = smass_ref[...]
    u_ref[...] = TEMP * (mass - LN2 * joined)
    shift = LOG2E * mass - joined
    for k in range(16):
        shift_row[:, k * 128 : k * 128 + 128] = jnp.broadcast_to(shift[k : k + 1, :], (8, 128))

    def col_copy(to):
        return pltpu.make_async_remote_copy(
            src_ref=col_mine.at[pl.ds(to // 2, 1)],
            dst_ref=col_lse.at[pl.ds(src, 1)],
            send_sem=send.at[3],
            recv_sem=col_recv.at[src],
            device_id={"src": to},
            device_id_type=MESH,
        )

    def half(h, _):
        def lanes(b, _):
            for g in range(64):
                down8 = pl.ds(pl.multiple_of(h * 1024 + b * 512 + g * 8, 8), 8)
                values = [
                    logits[down8, k * 128 : k * 128 + 128] + shift_row[:, k * 128 : k * 128 + 128]
                    for k in range(16)
                ]
                mark = tree(jnp.maximum, values)
                at = pl.ds(pl.multiple_of(b * 512 + g * 8, 8), 8)
                lane_peak[at, :] = mark
                lane_sum[at, :] = tree(jnp.add, [jnp.exp2(value - mark) for value in values])
            return 0

        lax.fori_loop(0, 2, lanes, 0)
        for q in range(8):
            at = slice(q * 128, q * 128 + 128)
            peaks, sums = lane_peak[at, :].T, lane_sum[at, :].T
            mark = jnp.max(peaks, axis=0, keepdims=True)
            col_mine[pl.ds(h * 8 + q, 1), :] = mark + jnp.log2(
                jnp.sum(sums * jnp.exp2(peaks - mark), axis=0, keepdims=True)
            )

        def col_push(k, _):
            to = h * 16 + k

            @pl.when(to != src)
            def _():
                col_copy(to).start()

            return 0

        lax.fori_loop(0, 16, col_push, 0)
        return 0

    lax.fori_loop(0, 2, half, 0)
    col_lse[pl.ds(src, 1), :] = col_mine[pl.ds(src // 2, 1), :]

    def col_wait(k, _):
        other = (src + k) % SRC
        pltpu.make_async_remote_copy(
            src_ref=col_mine.at[pl.ds(0, 1)],
            dst_ref=col_lse.at[pl.ds(other, 1)],
            send_sem=send.at[3],
            recv_sem=col_recv.at[other],
            device_id={"src": src},
            device_id_type=MESH,
        ).wait_recv()
        return 0

    lax.fori_loop(1, SRC, col_wait, 0)
    partial = col_lse[...]
    mark = jnp.max(partial, axis=0, keepdims=True)
    joined = mark + jnp.log2(jnp.sum(jnp.exp2(partial - mark), axis=0, keepdims=True))
    mine = jnp.where(core == 1, joined[:, 64:128], joined[:, 0:64])
    v_ref[...] = TEMP * (tmass_ref[...] - (LN2 * mine - INV_TEMP * own_pot))

    for k, (buffer, many) in enumerate(
        ((held, SRC - 1), (aux, SRC - 1), (row_lse, TGT - 1), (col_lse, SRC - 1))
    ):
        part = buffer.at[pl.ds(0, many)]
        pltpu.make_async_copy(part, part, send.at[k]).wait()


def per_device(src_codes, src_scales, log_source_mass, tgt_codes, tgt_scales, tgt_potential, log_target_mass):
    vmem = pl.BlockSpec(memory_space=pltpu.VMEM)
    u, v = pl.pallas_call(
        kernel,
        out_shape=(
            jax.ShapeDtypeStruct((16, 128), F32),
            jax.ShapeDtypeStruct((1, OWN), F32),
        ),
        in_specs=[vmem] * 7,
        out_specs=(vmem, vmem),
        scratch_shapes=[
            pltpu.VMEM((SRC, OWN, 256), BF16),
            pltpu.VMEM((SRC, 1, 384), F32),
            pltpu.VMEM((ROWS, 512), BF16),
            pltpu.VMEM((256, 512), BF16),
            pltpu.VMEM((ROWS, ROWS), F32),
            pltpu.VMEM((8, ROWS), F32),
            pltpu.VMEM((8, ROWS), F32),
            pltpu.VMEM((8, ROWS), F32),
            pltpu.VMEM((8, ROWS), F32),
            pltpu.VMEM((256, 128), F32),
            pltpu.VMEM((256, 128), F32),
            pltpu.VMEM((1024, 128), F32),
            pltpu.VMEM((1024, 128), F32),
            pltpu.VMEM((TGT, 16, 128), F32),
            pltpu.VMEM((16, 128), F32),
            pltpu.VMEM((SRC, 128), F32),
            pltpu.SemaphoreType.DMA((SRC,)),
            pltpu.SemaphoreType.DMA((SRC,)),
            pltpu.SemaphoreType.DMA((TGT,)),
            pltpu.SemaphoreType.DMA((SRC,)),
            pltpu.SemaphoreType.DMA((4,)),
        ],
        compiler_params=pltpu.CompilerParams(
            collective_id=0, has_side_effects=True, vmem_limit_bytes=44 << 20
        ),
        cost_estimate=pl.CostEstimate(
            flops=2 * ROWS * ROWS * 512, bytes_accessed=2 << 20, transcendentals=2 * ROWS * ROWS
        ),
    )(
        src_codes,
        src_scales.T,
        log_source_mass.reshape(16, 128),
        tgt_codes,
        tgt_scales.T,
        tgt_potential.reshape(1, OWN),
        log_target_mass.reshape(1, OWN),
    )
    return u.reshape(ROWS), v.reshape(OWN)


def solution(mesh):
    return jax.shard_map(
        per_device,
        mesh=mesh,
        in_specs=(
            P("src", None),
            P("src", None),
            P("src"),
            P(("tgt", "src"), None),
            P(("tgt", "src"), None),
            P(("tgt", "src")),
            P(("tgt", "src")),
        ),
        out_specs=(P("src"), P(("tgt", "src"))),
        check_vma=False,
    )
```

time: 185 us -> 55.2 us (0.30); the launches traced: 182 us -> 54.9 us
  waiting for transfers between devices: 49.4 us -> 0 us
  Pallas kernels: 0 us -> 49.1 us
  local copies, waits for them, and re-layouts: 40.5 us -> 5.12 us
  other arithmetic: 30.7 us -> 0 us
  matrix products: 24.2 us -> 0 us
  starting transfers between devices: 22.1 us -> 0 us
  blocking collectives: 13.3 us -> 0 us
    all_to_all x2 -> x0, waiting for transfers between devices: 49.4 us -> none  [from_everyone(): lax.all_to_all(jnp.broadcast_to(array[None], (length, *array.shape)), axi...]
    pallas_call x0 -> x1, Pallas kernels: none -> 49.1 us  [per_device(): pl.pallas_call(kernel, out_shape=(jax.ShapeDtypeStruct((16, 128), F32), j...]
    squeeze x32 -> x0, local copies, waits for them, and re-layouts: 27.2 us -> none  [per_device(): piece_max, piece_sum = lax.map(per_block, (code_blocks, scale_blocks))]
    dot_general x64 -> x0, matrix products: 24.2 us -> none  [block_scores(): lax.dot_general(source_codes[:, low_edge:low_edge + block_width], target_...]
    all_to_all x2 -> x0, starting transfers between devices: 22.1 us -> none  [from_everyone(): lax.all_to_all(jnp.broadcast_to(array[None], (length, *array.shape)), axi...]
    convert_element_type x33 -> x0, other arithmetic: 21.4 us -> none  [the longest x32 21 us: block_scores(): source_scales = source_scales.astype(jnp.float32)]
    all_to_all x1 -> x0, blocking collectives: 13.3 us -> none  [per_device(): lax.all_to_all(partial_lse.reshape(lax.axis_size('src'), own_count), 'src...]
    dynamic_update_slice x64 -> x0, local copies, waits for them, and re-layouts: 7.71 us -> none  [the longest x32 6.55 us: per_device(): lax.map(per_column_block, (code_blocks, scale_blocks, potential_blocks))]
  transfers between devices with their start and end apart: 2 -> 0, of which waited for: 2 -> 0; matrix products, arithmetic and copies ran while one was open for 0% -> 0% of each run, Pallas kernels for 0% -> 0%
where the time goes in v1:
time: 55.2 us; the launch traced here: 54.9 us
  Pallas kernels  49.1 us (89%)
  local copies, waits for them, and re-layouts  5.12 us (9%)
  between operations  0.67 us (1%)
    pallas_call x1, Pallas kernels, per_device(): pl.pallas_call(kernel, out_shape=(jax.ShapeDtypeStruct((16, 128), F32), j...  49.1 us
    unnamed x16, local copies, waits for them, and re-layouts  5.12 us

profile of v1, /device:TPU:1, one launch (start us, length us, event | category | flops | bytes accessed | tf_op | source)
XLA Modules:
  0.0 54.9 jit_solution(8896606019398396796)
XLA Ops:
  0.6 0.0 copy-start.2
  0.6 0.0 copy-start.4
  0.7 0.0 copy-start.5
  0.7 0.7 %copy-done.2 = bf16[2048,2]{0,1:T(2,128)(2,1)S(1)} copy-done((bf16[2048,2]{0,1:T(2,128)(2,1)S(1)}, bf16[2048,2]{0,1:T(2,128)(2,1)}, u32[]{:S(2)}) %copy-start.2) | copy-done | bytes 8216
  1.3 0.0 copy-done.4
  1.3 0.0 copy-done.5
  1.3 0.0 copy-start
  1.3 1.2 %copy-done = bf16[2048,256]{1,0:T(8,128)(2,1)S(1)} copy-done((bf16[2048,256]{1,0:T(8,128)(2,1)S(1)}, bf16[2048,256]{1,0:T(8,128)(2,1)}, u32[]{:S(2)}) %copy-start) | copy-done | bytes 1048600
  2.6 0.0 copy-start.1
  2.6 0.8 %copy-done.1 = bf16[64,256]{1,0:T(8,128)(2,1)S(1)} copy-done((bf16[64,256]{1,0:T(8,128)(2,1)S(1)}, bf16[64,256]{1,0:T(8,128)(2,1)}, u32[]{:S(2)}) %copy-start.1) | copy-done | bytes 32792
  3.3 0.0 copy-start.3
  3.3 0.7 %copy-done.3 = f32[2048]{0:T(1024)S(1)} copy-done((f32[2048]{0:T(1024)S(1)}, f32[2048]{0:T(1024)}, u32[]{:S(2)}) %copy-start.3) | copy-done | bytes 8216
  4.0 0.0 copy-start.6
  4.0 0.7 %copy-done.6 = f32[64]{0:T(128)S(1)} copy-done((f32[64]{0:T(128)S(1)}, f32[64]{0:T(128)}, u32[]{:S(2)}) %copy-start.6) | copy-done | bytes 280
  4.7 49.1 %shard_map.86 = (f32[16,128]{1,0:T(8,128)S(1)}, f32[1,64]{1,0:T(1,128)S(1)}) custom-call(bf16[2048,256]{1,0:T(8,128)(2,1)S(1)} %copy-done, bf16[2,2048]{1,0:T(2,128)(2,1)S(1)} %bitcast.8, f32[16,128]{1,0:T(8,128)S(1)} %bitcast.9, bf16[64,256]{1,0:T(8,128)(2,1)S(1)} %copy-done.1, bf16[2,64]{1,0:T(2,128)(2,1)S(1)} %bitcast.10, bf16[1,64]{1,0:T(2,128)(2,1)S(1)} %bitcast.11, ...), custom_call_target="tpu_custom_call" | custom-call | flops 4294967296 | bytes 2097152 | tf_op jit(solution)/shard_map/pallas_call | solution.py:390
  53.8 0.6 %copy.11 = f32[2048]{0:T(1024)} copy(f32[2048]{0:T(1024)S(1)} %bitcast.7) | data formatting | bytes 16384
  54.4 0.5 copy.12
Async XLA Ops:
  0.6 0.7 %copy-start.2 = (bf16[2048,2]{0,1:T(2,128)(2,1)S(1)}, bf16[2048,2]{0,1:T(2,128)(2,1)}, u32[]{:S(2)}) copy-start(bf16[2048,2]{0,1:T(2,128)(2,1)} %param.8) | copy-start | bytes 24580
  0.6 0.7 %copy-start.4 = (bf16[64,2]{0,1:T(2,128)(2,1)S(1)}, bf16[64,2]{0,1:T(2,128)(2,1)}, u32[]{:S(2)}) copy-start(bf16[64,2]{0,1:T(2,128)(2,1)} %param.11) | copy-start | bytes 772
  0.7 0.7 %copy-start.5 = (bf16[64]{0:T(256)(128)(2,1)S(1)}, bf16[64]{0:T(256)(128)(2,1)}, u32[]{:S(2)}) copy-start(bf16[64]{0:T(256)(128)(2,1)} %param.12) | copy-start | bytes 388
  1.3 1.2 %copy-start = (bf16[2048,256]{1,0:T(8,128)(2,1)S(1)}, bf16[2048,256]{1,0:T(8,128)(2,1)}, u32[]{:S(2)}) copy-start(bf16[2048,256]{1,0:T(8,128)(2,1)} %codes_ref.1) | copy-start | bytes 3145732
  2.6 0.8 %copy-start.1 = (bf16[64,256]{1,0:T(8,128)(2,1)S(1)}, bf16[64,256]{1,0:T(8,128)(2,1)}, u32[]{:S(2)}) copy-start(bf16[64,256]{1,0:T(8,128)(2,1)} %tcodes_ref.1) | copy-start | bytes 98308
  3.3 0.7 %copy-start.3 = (f32[2048]{0:T(1024)S(1)}, f32[2048]{0:T(1024)}, u32[]{:S(2)}) copy-start(f32[2048]{0:T(1024)} %param.9) | copy-start | bytes 24580
  4.0 0.7 %copy-start.6 = (f32[64]{0:T(128)S(1)}, f32[64]{0:T(128)}, u32[]{:S(2)}) copy-start(f32[64]{0:T(128)} %param.13) | copy-start | bytes 772

commit v2 on v1

--- a/solution.py
+++ b/solution.py
@@ -50,15 +50,21 @@
 
 
 def kernel(
+    codes_hbm,
+    sscale_hbm,
+    smass_hbm,
+    tcodes_hbm,
+    tscale_hbm,
+    tpot_hbm,
+    tmass_hbm,
+    u_ref,
+    v_ref,
     codes_ref,
     sscale_ref,
     smass_ref,
-    tcodes_ref,
     tscale_ref,
     tpot_ref,
     tmass_ref,
-    u_ref,
-    v_ref,
     held,
     aux,
     left,
@@ -80,13 +86,14 @@
     row_recv,
     col_recv,
     send,
+    local,
 ):
     src = lax.axis_index("src")
     tgt = lax.axis_index("tgt")
-    z, x, core = src // 4, (src // 2) % 2, src % 2
+    z, x, core = src // 4, (src // 2) & 1, src & 1
 
     def slot(zz, xx, cc):
-        return ((zz + 2 * ZS) % ZS) * 4 + xx * 2 + cc
+        return (zz & (ZS - 1)) * 4 + xx * 2 + cc
 
     def codes_copy(piece, to):
         return pltpu.make_async_remote_copy(
@@ -116,27 +123,43 @@
         codes_copy(piece, src).wait_recv()
         aux_copy(piece, src).wait_recv()
 
-    up, down = slot(z + 1, x, core), slot(z - 1, x, core)
     partner, sibling = slot(z, 1 - x, core), slot(z, x, 1 - core)
 
     barrier = pltpu.get_barrier_semaphore()
 
     def greet_src(k, _):
         pl.semaphore_signal(
-            barrier, inc=1, device_id={"src": (src + k) % SRC}, device_id_type=MESH
+            barrier, inc=1, device_id={"src": (src + k) & (SRC - 1)}, device_id_type=MESH
         )
         return 0
 
     def greet_tgt(k, _):
         pl.semaphore_signal(
-            barrier, inc=1, device_id={"tgt": (tgt + k) % TGT}, device_id_type=MESH
+            barrier, inc=1, device_id={"tgt": (tgt + k) & (TGT - 1)}, device_id_type=MESH
         )
         return 0
 
     lax.fori_loop(1, SRC, greet_src, 0)
     lax.fori_loop(1, TGT, greet_tgt, 0)
 
-    held[src] = tcodes_ref[...]
+    fetches = [
+        pltpu.make_async_copy(a, b, local.at[k])
+        for k, (a, b) in enumerate(
+            (
+                (tcodes_hbm, held.at[src]),
+                (tscale_hbm, tscale_ref),
+                (tpot_hbm, tpot_ref),
+                (sscale_hbm, sscale_ref),
+                (codes_hbm, codes_ref),
+                (smass_hbm, smass_ref),
+                (tmass_hbm, tmass_ref),
+            )
+        )
+    ]
+    for fetch in fetches:
+        fetch.start()
+    for fetch in fetches[:3]:
+        fetch.wait()
     own_scale = tscale_ref[...].astype(F32)
     own_pot = tpot_ref[...].astype(F32)
     blank = jnp.zeros((1, OWN), F32)
@@ -146,10 +169,14 @@
 
     pl.semaphore_wait(barrier, SRC + TGT - 2)
 
-    push(src, up)
-    push(src, down)
+    push(src, sibling)
+    push(src, slot(z + 1, x, core))
+    push(src, slot(z - 1, x, core))
     push(src, partner)
-    push(src, sibling)
+    for away in (2, -2, 3, -3, 4):
+        push(src, slot(z + away, x, core))
+    for fetch in fetches[3:]:
+        fetch.wait()
 
     source_scale = sscale_ref[...].astype(F32)
 
@@ -170,75 +197,61 @@
         left[at, 256:384] = high
         left[at, 384:512] = (scaled - high.astype(F32)).astype(BF16)
 
+    def own_column(*steps):
+        for step in steps:
+            piece = slot(z + step, x, core)
+            arrived(piece)
+            push(piece, partner)
+            push(piece, sibling)
+
+    def other_column(*steps):
+        for step in steps:
+            piece = slot(z + step, 1 - x, core)
+            arrived(piece)
+            push(piece, sibling)
+
     source_part(0, 8)
-
-    arrived(partner)
-    push(partner, up)
-    push(partner, down)
-    push(partner, sibling)
-    for side, onward in ((-1, up), (1, down)):
-        piece = slot(z + side, x, core)
-        arrived(piece)
-        push(piece, onward)
-        push(piece, sibling)
-
+    other_column(0)
+    own_column(1, -1)
     source_part(8, 16)
     scale_row[...] = jnp.broadcast_to(source_scale[0:1] * (INV_TEMP * LOG2E / 16.0), (8, ROWS))
     peak[...] = jnp.full((8, ROWS), -1e30, F32)
     total[...] = jnp.zeros((8, ROWS), F32)
-
-    for side, onward in ((-1, up), (1, down)):
-        piece = slot(z + side, 1 - x, core)
-        arrived(piece)
-        push(piece, onward)
-        push(piece, sibling)
+    own_column(2, -2)
 
     def chunk(k, _):
-        far = (k + 1) // 2 + 1
-        own_column = k % 2 == 1
-
-        @pl.when(jnp.logical_and(k >= 1, k <= 2))
+        @pl.when(k == 1)
         def _():
-            xx = jnp.where(own_column, x, 1 - x)
-            for side, onward in ((-1, up), (1, down)):
-                piece = slot(z + side * 2, xx, core)
-                arrived(piece)
-                push(piece, onward)
-                push(piece, sibling)
-
-        @pl.when(jnp.logical_and(k >= 3, k <= 4))
+            own_column(3, -3)
+
+        @pl.when(k == 2)
         def _():
-            xx = jnp.where(own_column, x, 1 - x)
-            for side, onward in ((-1, up), (1, down)):
-                piece = slot(z + side * 3, xx, core)
-                arrived(piece)
-
-                @pl.when(own_column if side == -1 else jnp.logical_not(own_column))
-                def _():
-                    push(piece, onward)
-
-                push(piece, sibling)
+            own_column(4)
+
+        @pl.when(jnp.logical_and(k >= 2, k <= 4))
+        def _():
+            other_column(k - 1, 1 - k)
 
         @pl.when(k == 5)
         def _():
-            for xx in (x, 1 - x):
-                piece = slot(z + 4, xx, core)
-                arrived(piece)
-                push(piece, sibling)
-
-        away = (k + 1) // 2
-        zz = (z + jnp.where(k % 2 == 1, away, -away) + 2 * ZS) % ZS
-        for xx in (0, 1):
-            arrived(slot(zz, xx, 1 - core))
-
-        first = pl.multiple_of(zz * 256, 256)
-        side_rows = [aux[zz * 4 + p] for p in range(4)]
+            other_column(4)
+
+        away = jnp.where(k >= 4, k - 3, k)
+        beside = jnp.logical_or(k == 0, k == 7)
+        x_a = jnp.where(jnp.logical_and(k >= 4, k <= 6), 1 - x, x)
+        x_b = jnp.where(beside, 1 - x, x_a)
+        z_b = jnp.where(beside, z + away, z - away)
+        chips = (slot(z + away, x_a, 0), slot(z_b, x_b, 0))
+        for chip in chips:
+            arrived(chip + 1 - core)
+
+        side_rows = [aux[chip + c] for chip in chips for c in (0, 1)]
         wide = replicate(
             [(row[:, b * 128 : b * 128 + 128], OWN) for b in range(3) for row in side_rows]
         )
         t_scale[...] = wide[0:256]
         t_pot[...] = wide[512:768] * (INV_TEMP * LOG2E)
-        pieces = held[pl.ds(zz * 4, 4)].reshape(256, 256)
+        pieces = jnp.concatenate([held[pl.ds(chip, 2)].reshape(128, 256) for chip in chips])
         scaled = pieces[:, 128:256].astype(F32) * (wide[256:512] / wide[0:256])
         high = scaled.astype(BF16)
         right[:, 0:128] = pieces[:, 0:128]
@@ -261,7 +274,8 @@
                     scale, pot = t_scale[down8, :], t_pot[down8, :]
                     for i, t in enumerate(tiles):
                         value = product[down8, i * 128 : i * 128 + 128] * s_scale[i] * scale + pot
-                        logits[pl.ds(first + g * 8, 8), t] = value
+                        at = pl.multiple_of(chips[g // 16] * OWN + (g % 16) * 8, 8)
+                        logits[pl.ds(at, 8), t] = value
                         values[i].append(value)
                 for i in range(2):
                     mark = jnp.maximum(high_mark[i], tree(jnp.maximum, values[i]))
@@ -291,15 +305,14 @@
             device_id_type=MESH,
         )
 
-    def row_push(k, _):
-        row_copy(tgt, (tgt + k) % TGT).start()
-        return 0
+    others = [(a, b) for a in (0, 1) for b in range(ZS) if a or b]
+    for a, b in sorted(others, key=lambda ab: -2 * ab[0] - min(ab[1], ZS - ab[1])):
+        row_copy(tgt, ((tgt // ZS) ^ a) * ZS + ((tgt + b) & (ZS - 1))).start()
 
     def row_wait(k, _):
-        row_copy((tgt + k) % TGT, tgt).wait_recv()
-        return 0
-
-    lax.fori_loop(1, TGT, row_push, 0)
+        row_copy((tgt + k) & (TGT - 1), tgt).wait_recv()
+        return 0
+
     lax.fori_loop(1, TGT, row_wait, 0)
 
     every = [row_lse[g] for g in range(TGT)]
@@ -322,30 +335,33 @@
         )
 
     def half(h, _):
+        def place(n):
+            return (z + 2 + h * 4 + n) & (ZS - 1)
+
         def lanes(b, _):
-            for g in range(64):
-                down8 = pl.ds(pl.multiple_of(h * 1024 + b * 512 + g * 8, 8), 8)
+            for g in range(32):
+                down8 = pl.ds(pl.multiple_of(place(b) * 256 + g * 8, 8), 8)
                 values = [
                     logits[down8, k * 128 : k * 128 + 128] + shift_row[:, k * 128 : k * 128 + 128]
                     for k in range(16)
                 ]
                 mark = tree(jnp.maximum, values)
-                at = pl.ds(pl.multiple_of(b * 512 + g * 8, 8), 8)
+                at = pl.ds(pl.multiple_of(b * 256 + g * 8, 8), 8)
                 lane_peak[at, :] = mark
                 lane_sum[at, :] = tree(jnp.add, [jnp.exp2(value - mark) for value in values])
             return 0
 
-        lax.fori_loop(0, 2, lanes, 0)
+        lax.fori_loop(0, 4, lanes, 0)
         for q in range(8):
             at = slice(q * 128, q * 128 + 128)
             peaks, sums = lane_peak[at, :].T, lane_sum[at, :].T
             mark = jnp.max(peaks, axis=0, keepdims=True)
-            col_mine[pl.ds(h * 8 + q, 1), :] = mark + jnp.log2(
+            col_mine[pl.ds(place(q // 2) * 2 + q % 2, 1), :] = mark + jnp.log2(
                 jnp.sum(sums * jnp.exp2(peaks - mark), axis=0, keepdims=True)
             )
 
         def col_push(k, _):
-            to = h * 16 + k
+            to = place(k // 4) * 4 + ((src + k) & 3)
 
             @pl.when(to != src)
             def _():
@@ -360,7 +376,7 @@
     col_lse[pl.ds(src, 1), :] = col_mine[pl.ds(src // 2, 1), :]
 
     def col_wait(k, _):
-        other = (src + k) % SRC
+        other = (src + k) & (SRC - 1)
         pltpu.make_async_remote_copy(
             src_ref=col_mine.at[pl.ds(0, 1)],
             dst_ref=col_lse.at[pl.ds(other, 1)],
@@ -393,9 +409,15 @@
             jax.ShapeDtypeStruct((16, 128), F32),
             jax.ShapeDtypeStruct((1, OWN), F32),
         ),
-        in_specs=[vmem] * 7,
+        in_specs=[pl.BlockSpec(memory_space=pltpu.HBM)] * 7,
         out_specs=(vmem, vmem),
         scratch_shapes=[
+            pltpu.VMEM((ROWS, 256), BF16),
+            pltpu.VMEM((2, ROWS), BF16),
+            pltpu.VMEM((16, 128), F32),
+            pltpu.VMEM((2, OWN), BF16),
+            pltpu.VMEM((1, OWN), BF16),
+            pltpu.VMEM((1, OWN), F32),
             pltpu.VMEM((SRC, OWN, 256), BF16),
             pltpu.VMEM((SRC, 1, 384), F32),
             pltpu.VMEM((ROWS, 512), BF16),
@@ -417,9 +439,10 @@
             pltpu.SemaphoreType.DMA((TGT,)),
             pltpu.SemaphoreType.DMA((SRC,)),
             pltpu.SemaphoreType.DMA((4,)),
+            pltpu.SemaphoreType.DMA((7,)),
         ],
         compiler_params=pltpu.CompilerParams(
-            collective_id=0, has_side_effects=True, vmem_limit_bytes=44 << 20
+            collective_id=0, has_side_effects=True, vmem_limit_bytes=62 << 20
         ),
         cost_estimate=pl.CostEstimate(
             flops=2 * ROWS * ROWS * 512, bytes_accessed=2 << 20, transcendentals=2 * ROWS * ROWS

time: 55.2 us -> 50.9 us (0.922)
  local copies, waits for them, and re-layouts: 5.12 us -> 1.81 us
  Pallas kernels: 49.1 us -> 48.3 us
    unnamed x16 -> x4, local copies, waits for them, and re-layouts: 5.12 us -> 1.81 us
    pallas_call x1, Pallas kernels: 49.1 us -> 48.3 us  [per_device(): pl.pallas_call(kernel, out_shape=(jax.ShapeDtypeStruct((16, 128), F32), j...]
where the time goes in v2:
time: 50.9 us; the launch traced here: 50.8 us
  Pallas kernels  48.3 us (95%)
  local copies, waits for them, and re-layouts  1.81 us (4%)
  between operations  0.65 us (1%)
    pallas_call x1, Pallas kernels, per_device(): pl.pallas_call(kernel, out_shape=(jax.ShapeDtypeStruct((16, 128), F32), j...  48.3 us
    unnamed x4, local copies, waits for them, and re-layouts  1.81 us

profile of v2, /device:TPU:1, one launch (start us, length us, event | category | flops | bytes accessed | tf_op | source)
XLA Modules:
  0.0 50.8 jit_solution(248031650930516859)
XLA Ops:
  0.6 48.3 %shard_map.86 = (f32[16,128]{1,0:T(8,128)}, f32[1,64]{1,0:T(1,128)}) custom-call(bf16[2048,256]{1,0:T(8,128)(2,1)} %codes_hbm.1, bf16[2,2048]{1,0:T(2,128)(2,1)} %bitcast.8, f32[16,128]{1,0:T(8,128)} %bitcast.9, bf16[64,256]{1,0:T(8,128)(2,1)} %tcodes_hbm.1, bf16[2,64]{1,0:T(2,128)(2,1)} %bitcast.10, bf16[1,64]{1,0:T(2,128)(2,1)} %bitcast.11, f32[1,64]{1,0:T(1,128)} %bitcast.12), custom_call_target="tpu_custom_call" | custom-call | flops 4294967296 | bytes 2097152 | tf_op jit(solution)/shard_map/pallas_call | solution.py:406
  48.9 0.0 copy-start
  48.9 1.3 %copy.11 = f32[2048]{0:T(1024)} copy(f32[2048]{0:T(1024)} %bitcast.7) | data formatting | bytes 16384
  50.2 0.0 copy-done
  50.2 0.5 %copy.12 = f32[64]{0:T(128)} copy(f32[64]{0:T(128)S(1)} %bitcast.13) | data formatting | bytes 512
Async XLA Ops:
  48.9 1.3 %copy-start = (f32[1,64]{1,0:T(1,128)S(1)}, f32[1,64]{1,0:T(1,128)}, u32[]{:S(2)}) copy-start(f32[1,64]{1,0:T(1,128)} %get-tuple-element.5) | copy-start | bytes 772

commit v3 on v2

--- a/solution.py
+++ b/solution.py
@@ -127,11 +127,8 @@
 
     barrier = pltpu.get_barrier_semaphore()
 
-    def greet_src(k, _):
-        pl.semaphore_signal(
-            barrier, inc=1, device_id={"src": (src + k) & (SRC - 1)}, device_id_type=MESH
-        )
-        return 0
+    def greet(other):
+        pl.semaphore_signal(barrier, inc=1, device_id={"src": other}, device_id_type=MESH)
 
     def greet_tgt(k, _):
         pl.semaphore_signal(
@@ -139,8 +136,10 @@
         )
         return 0
 
-    lax.fori_loop(1, SRC, greet_src, 0)
+    near = [slot(z + away, x, core) for away in (4, 3, -3, 2, -2, 1, -1)] + [partner, sibling]
     lax.fori_loop(1, TGT, greet_tgt, 0)
+    for other in near:
+        greet(other)
 
     fetches = [
         pltpu.make_async_copy(a, b, local.at[k])
@@ -167,7 +166,7 @@
         [own_scale[0:1], blank, own_scale[1:2], blank, own_pot, blank], axis=1
     )
 
-    pl.semaphore_wait(barrier, SRC + TGT - 2)
+    pl.semaphore_wait(barrier, len(near) + TGT - 1)
 
     push(src, sibling)
     push(src, slot(z + 1, x, core))

time: 50.9 us -> 50.6 us (level)
  no operation moved by 1% of the time
where the time goes in v3:
time: 50.6 us; the launch traced here: 50.5 us
  Pallas kernels  48 us (95%)
  local copies, waits for them, and re-layouts  1.81 us (4%)
  between operations  0.65 us (1%)
    pallas_call x1, Pallas kernels, per_device(): pl.pallas_call(kernel, out_shape=(jax.ShapeDtypeStruct((16, 128), F32), j...  48 us
    unnamed x4, local copies, waits for them, and re-layouts  1.81 us

profile of v3, /device:TPU:1, one launch (start us, length us, event | category | flops | bytes accessed | tf_op | source)
XLA Modules:
  0.0 50.5 jit_solution(1280111582917170373)
XLA Ops:
  0.6 48.0 %shard_map.86 = (f32[16,128]{1,0:T(8,128)}, f32[1,64]{1,0:T(1,128)}) custom-call(bf16[2048,256]{1,0:T(8,128)(2,1)} %codes_hbm.1, bf16[2,2048]{1,0:T(2,128)(2,1)} %bitcast.8, f32[16,128]{1,0:T(8,128)} %bitcast.9, bf16[64,256]{1,0:T(8,128)(2,1)} %tcodes_hbm.1, bf16[2,64]{1,0:T(2,128)(2,1)} %bitcast.10, bf16[1,64]{1,0:T(2,128)(2,1)} %bitcast.11, f32[1,64]{1,0:T(1,128)} %bitcast.12), custom_call_target="tpu_custom_call" | custom-call | flops 4294967296 | bytes 2097152 | tf_op jit(solution)/shard_map/pallas_call | solution.py:405
  48.6 0.0 copy-start
  48.6 1.3 %copy.11 = f32[2048]{0:T(1024)} copy(f32[2048]{0:T(1024)} %bitcast.7) | data formatting | bytes 16384
  49.9 0.0 copy-done
  49.9 0.5 %copy.12 = f32[64]{0:T(128)} copy(f32[64]{0:T(128)S(1)} %bitcast.13) | data formatting | bytes 512
Async XLA Ops:
  48.6 1.3 %copy-start = (f32[1,64]{1,0:T(1,128)S(1)}, f32[1,64]{1,0:T(1,128)}, u32[]{:S(2)}) copy-start(f32[1,64]{1,0:T(1,128)} %get-tuple-element.5) | copy-start | bytes 772
